TPU v7x, 32 devices: a whole 2x2x4 slice. The times are simulated.
32 devices in a mesh: ctx: 8 (over z, x), head: 4 (over y, core).
Axes of the slice: x: 2, y: 2, z: 4, core: 2. Of those that a mesh axis runs over, the one named last changes fastest.
Arguments:
- asking_vectors: bfloat16 [4096, 2048], P('ctx', 'head'), may hold values from -6 to 6
- lookup_vectors: bfloat16 [4096, 2048], P('ctx', 'head'), may hold values from -16 to 16
- payload_vectors: bfloat16 [4096, 2048], P('ctx', 'head'), may hold values from -16 to 16
- segment_owner_ids: int32 [16], P('ctx'), may hold values from 0 to 3, never falling along the last dimension, each value on 1 to 12 neighbouring positions
- attender_logit_factor: float32 [16], P('head'), may hold values from 4 to 16
- tier_logit_shift: float32 [16], P('head'), may hold values from -0.2 to 0.4
- final_projection_weights: bfloat16 [2048, 4096], P('head'), may hold values from -0.125 to 0.125
Outputs:
- mixed: bfloat16 [4096, 4096], P('ctx', 'head')
All inputs are finite; a program needn't handle non-finite values.
Results may differ from a plain program's by a relative error of at most 0.011.
Values may be sent and summed in bfloat16 or wider, within the bound.
A program may use at most 64 MiB of HBM per device.

v0:
```python
import jax
import jax.numpy as jnp
from jax import lax
from jax.sharding import PartitionSpec as P

EPS = 1e-06


def swapped(block, axis, distance):
    count = lax.axis_size(axis)
    route = []
    for low in range(count):
        high = low | 1 << distance
        if high != low and high < count:
            route += [(low, high), (high, low)]
    return lax.ppermute(block, axis, route)


def unit_rows(matrix):
    return matrix * lax.rsqrt(jnp.mean(matrix * matrix, axis=-1, keepdims=True) + EPS)


def run_means(matrix, attender_dimension):
    shaped = matrix.reshape(
        (matrix.shape[0] // attender_dimension, attender_dimension) + matrix.shape[1:]
    )
    return jnp.mean(shaped, axis=1)


def span_means(stacked, attender_dimension):
    shaped = stacked.reshape(
        stacked.shape[0],
        stacked.shape[1] // attender_dimension,
        attender_dimension,
        stacked.shape[2],
        stacked.shape[3],
    )
    return jnp.mean(shaped, axis=2)


def flip_pairs(matrix):
    shaped = matrix.reshape((matrix.shape[0] // 2, 2) + matrix.shape[1:])
    return shaped[:, ::-1].reshape(matrix.shape)


def attend(query_unit, key_rows, value_rows, logit_multiplier, offset, keep, numer, denom):
    groups = key_rows.shape[0]
    grouped = query_unit.reshape((groups, query_unit.shape[0] // groups) + query_unit.shape[1:])
    scores = jnp.einsum("gqhd,gkhd->ghqk", grouped, key_rows, preferred_element_type=jnp.float32)
    weights = jnp.exp(scores * logit_multiplier[:, None, None] + offset[:, None, None]) * keep
    totals = jnp.swapaxes(jnp.sum(weights, axis=-1), 1, 2).reshape(denom.shape)
    update = jnp.einsum(
        "ghqk,gkhd->gqhd",
        weights.astype(jnp.bfloat16),
        value_rows,
        preferred_element_type=jnp.float32,
    )
    return (numer + update.reshape(numer.shape), denom + totals)


def per_device(
    asking_vectors,
    lookup_vectors,
    payload_vectors,
    segment_owner_ids,
    attender_logit_factor,
    tier_logit_shift,
    final_projection_weights,
):
    rows = asking_vectors.shape[0]
    attender_count = attender_logit_factor.shape[0]
    attender_dimension = asking_vectors.shape[1] // attender_count
    blocks = segment_owner_ids.shape[0]
    block_rows = rows // blocks
    local_levels = blocks.bit_length() - 1
    q_unit = unit_rows(
        asking_vectors.astype(jnp.float32).reshape(rows, attender_count, attender_dimension)
    ).astype(jnp.bfloat16)
    k_unit = unit_rows(
        lookup_vectors.astype(jnp.float32).reshape(rows, attender_count, attender_dimension)
    )
    v_rows = payload_vectors.reshape(rows, attender_count, attender_dimension)
    v_wide = v_rows.astype(jnp.float32)
    logit_multiplier = attender_logit_factor / attender_dimension
    numer = jnp.zeros((rows, attender_count, attender_dimension), jnp.float32)
    denom = jnp.zeros((rows, attender_count), jnp.float32)
    still = jnp.zeros_like(tier_logit_shift)
    near_keys = k_unit.astype(jnp.bfloat16).reshape(
        blocks, block_rows, attender_count, attender_dimension
    )
    near_values = v_rows.reshape(blocks, block_rows, attender_count, attender_dimension)
    numer, denom = attend(
        q_unit, near_keys, near_values, logit_multiplier, still, 1.0, numer, denom
    )
    keep = (segment_owner_ids == flip_pairs(segment_owner_ids)).astype(jnp.float32)[
        :, None, None, None
    ]
    numer, denom = attend(
        q_unit,
        flip_pairs(near_keys),
        flip_pairs(near_values),
        logit_multiplier,
        still,
        keep,
        numer,
        denom,
    )
    ctx_levels = lax.axis_size("ctx").bit_length() - 1
    place = lax.axis_index("ctx")

    def far_attend(summary, level, numer, denom):
        rounded = summary.astype(jnp.bfloat16)
        return attend(
            q_unit,
            rounded[0:1],
            rounded[1:2],
            logit_multiplier,
            -level * tier_logit_shift,
            1.0,
            numer,
            denom,
        )

    base = jnp.stack([run_means(k_unit, blocks), run_means(v_wide, blocks)])
    split = ctx_levels // 2
    piece_rows = block_rows // 2**split
    piece = jnp.stack(
        [run_means(k_unit, rows // piece_rows), run_means(v_wide, rows // piece_rows)]
    )
    everyone = lax.all_gather(piece.astype(jnp.bfloat16), "ctx", axis=1, tiled=True).astype(
        piece.dtype
    )
    mine = base
    partner_numer = numer
    partner_denom = denom
    for partner_step in range(split):
        other = swapped(mine.astype(jnp.bfloat16), "ctx", partner_step).astype(mine.dtype)
        partner_numer, partner_denom = far_attend(
            other, local_levels + partner_step, partner_numer, partner_denom
        )
        if partner_step + 1 < split:
            lower = place >> partner_step & 1 == 0
            first = jnp.where(lower, mine, other)
            second = jnp.where(lower, other, mine)
            mine = span_means(jnp.concatenate([first, second], axis=1), 2)
    numer = partner_numer
    denom = partner_denom
    for step in range(split, ctx_levels):
        members = 2**step
        first_row = ((place >> step ^ 1) << step) * piece_rows
        sibling = lax.dynamic_slice_in_dim(everyone, first_row, members * piece_rows, 1)
        summary = span_means(sibling, 2 ** (step - split))
        numer, denom = far_attend(summary, local_levels + step, numer, denom)
    attended = (
        (numer / denom[:, :, None])
        .astype(jnp.bfloat16)
        .reshape(rows, attender_count * attender_dimension)
    )
    terms = jnp.dot(attended, final_projection_weights, preferred_element_type=jnp.float32)
    mixed = lax.psum_scatter(terms.astype(jnp.bfloat16), "head", scatter_dimension=1, tiled=True)
    return mixed


def solution(mesh):
    placed = (
        P("ctx", "head"),
        P("ctx", "head"),
        P("ctx", "head"),
        P("ctx"),
        P("head"),
        P("head"),
        P("head", None),
    )
    return jax.shard_map(
        per_device, mesh=mesh, in_specs=placed, out_specs=P("ctx", "head"), check_vma=False
    )
```

profile of v0, /device:TPU:0, one launch (start us, length us, event | category | flops | bytes accessed | tf_op | source)
XLA Modules:
  0.0 153.0 jit_solution(8324565900146109348)
XLA Ops:
  6.5 1.4 reshape.287
  8.0 2.2 %convert_multiply_fusion = f32[512,512]{1,0:T(8,128)} fusion(bf16[512,512]{1,0:T(8,128)(2,1)} %param.8), kind=kLoop, calls=%fused_computation.75 | loop fusion | flops 524288 | bytes 1572864 | tf_op jit(solution)/shard_map/mul | solution.py:20
  10.9 1.6 %mul.120 = f32[512,4,128]{2,1,0:T(4,128)S(1)} reshape(f32[512,512]{1,0:T(8,128)} %convert_multiply_fusion) | data formatting | bytes 2097152 | tf_op jit(solution)/shard_map/mul | solution.py:20
  17.9 2.9 %collective-permute-start = (bf16[2,256,4,128]{3,1,2,0:T(8,128)(2,1)}, bf16[2,256,4,128]{3,1,2,0:T(8,128)(2,1)}, u32[]{:S(2)}, u32[]{:S(2)}) collective-permute-start(bf16[2,256,4,128]{3,1,2,0:T(8,128)(2,1)} %pad_maximum_fusion), channel_id=1, source_target_pairs={{0,4},{4,0},{8,12},{12,8},{16,20},{20,16},{24,28},{28,24},{1,5},{5... | collective-permute-start | bytes 1572872 | tf_op jit(solution)/shard_map/ppermute | solution.py:16
  22.9 1.6 %reshape.276 = f32[2,256,4,128]{1,0,3,2:T(2,128)} reshape(bf16[512,512]{0,1:T(8,128)(2,1)S(1)} %copy.109) | data formatting | bytes 1572864 | tf_op jit(solution)/shard_map/reshape | solution.py:77
  25.0 1.3 reshape.278
  28.3 1.5 copy.112
  29.7 1.3 copy.125
  33.5 1.6 %fusion.34 = f32[2,4,256,256]{2,3,1,0:T(8,128)S(1)} fusion(f32[2,256,4,128]{3,2,1,0:T(4,128)S(1)} %copy-done.4, f32[2,256,4]{1,2,0:T(4,128)S(1)} %copy.113, f32[2,256,4,128]{3,1,2,0:T(8,128)S(1)} %copy.112, f32[2,256,4]{1,2,0:T(4,128)S(1)} %copy.111), kind=kOutput, calls=%fused_computation.47 | convolution fusion | flops 135266304 | bytes 4210688 | tf_op jit(solution)/shard_map/gqhd,gkhd->ghqk/dot_general | solution.py:49
  37.6 1.7 %copy.121 = f32[2,256,4,128]{3,2,1,0:T(4,128)} copy(f32[2,256,4,128]{3,1,2,0:T(8,128)S(1)} %fusion.10) | data formatting | bytes 2097152 | tf_op jit(solution)/shard_map/add | solution.py:58
  39.6 29.8 %all-gather.2.cloned.1.call-done = bf16[2,1024,4,128]{3,1,2,0:T(8,128)(2,1)} async-done(((bf16[2,128,4,128]{3,1,2,0:T(8,128)(2,1)}), bf16[2,1024,4,128]{3,1,2,0:T(8,128)(2,1)}) %all-gather.2.cloned.1.call-update) | async-done | bytes 2097168 | tf_op jit(solution)/shard_map/all_gather | solution.py:130
  69.4 1.9 %convert_element_type.97 = f32[2,1024,4,128]{3,1,2,0:T(8,128)S(1)} convert(bf16[2,1024,4,128]{3,1,2,0:T(8,128)(2,1)} %all-gather.2.cloned.1.call-done) | non-fusion elementwise | flops 1048576 | bytes 6291456 | tf_op jit(solution)/shard_map/convert_element_type | solution.py:130
  71.6 3.9 %reduce_sum.124 = f32[2,256,4,128]{3,1,2,0:T(8,128)} reduce(f32[2,256,2,4,128]{4,2,1,3,0:T(2,128)S(1)} %bitcast.108, f32[]{:T(128)} %constant.15.clone.1), dimensions={2}, to_apply=%region_6.0 | reduce | flops 262144 | bytes 3145732 | tf_op jit(solution)/shard_map/reduce_sum | solution.py:38
  75.4 1.3 multiply_convert_fusion
  77.2 1.5 %fusion.11 = f32[4,128,512]{2,1,0:T(8,128)} fusion(f32[4,512,256]{1,2,0:T(8,128)S(1)} %fusion.46, f32[4]{0:T(128)S(1)} %get-tuple-element.10, f32[4]{0:T(128)S(1)} %get-tuple-element.15, bf16[2,256,4,128]{3,1,2,0:T(8,128)(2,1)S(1)} %multiply_convert_fusion), kind=kOutput, calls=%fused_computation.18 | convolution fusion | flops 135790592 | bytes 3408896 | tf_op jit(solution)/shard_map/ghqk,gkhd->gqhd/dot_general | solution.py:52
  78.7 2.6 %copy.138 = f32[512,512]{1,0:T(8,128)} copy(f32[512,512]{0,1:T(8,128)} %bitcast.111) | data formatting | bytes 2097152 | tf_op jit(solution)/shard_map/reshape | solution.py:58
  81.7 1.3 copy-done
  83.1 1.5 %fusion.13 = f32[4,128,512]{2,1,0:T(8,128)} fusion(f32[4,512,256]{1,2,0:T(8,128)S(1)} %fusion.47, f32[4]{0:T(128)S(1)} %get-tuple-element.12, f32[4]{0:T(128)S(1)} %get-tuple-element.15, bf16[2,256,4,128]{3,1,2,0:T(8,128)(2,1)S(1)} %dynamic-slice_convert_fusion), kind=kOutput, calls=%fused_computation.19 | convolution fusion | flops 135790592 | bytes 3408896 | tf_op jit(solution)/shard_map/ghqk,gkhd->gqhd/dot_general | solution.py:52
  84.6 2.6 %copy.135 = f32[512,512]{1,0:T(8,128)} copy(f32[512,512]{0,1:T(8,128)} %bitcast.112) | data formatting | bytes 2097152 | tf_op jit(solution)/shard_map/reshape | solution.py:58
  87.2 4.2 %fusion.4 = (f32[4,512]{1,0:T(4,128)S(1)}, f32[4,512]{1,0:T(4,128)S(1)}, f32[4,512]{1,0:T(4,128)S(1)}, f32[4,512,256]{1,2,0:T(8,128)}) fusion(f32[4]{0:T(128)S(1)} %get-tuple-element.11, f32[4]{0:T(128)S(1)} %get-tuple-element.15, f32[4]{0:T(128)S(1)} %get-tuple-element.12, f32[4,512,256]{1,2,0:T(8,128)} %copy-done, f32[4]{0:T(128)S(1)} %get-tuple-element.10, ...), kind=kOutput, calls=%fused_computation.10 | convolution fusion | flops 138930176 | bytes 7102528 | tf_op jit(solution)/shard_map/gqhd,gkhd->ghqk/dot_general | solution.py:49
  91.6 2.3 %fusion.15 = f32[4,128,512]{2,1,0:T(8,128)S(1)} fusion(f32[4,512,256]{1,2,0:T(8,128)} %get-tuple-element.13, f32[4]{0:T(128)S(1)} %get-tuple-element.11, f32[4]{0:T(128)S(1)} %get-tuple-element.15, bf16[2,256,4,128]{3,1,2,0:T(8,128)(2,1)} %collective-permute-done), kind=kOutput, calls=%fused_computation.20 | convolution fusion | flops 135790592 | bytes 3407904 | tf_op jit(solution)/shard_map/ghqk,gkhd->gqhd/dot_general | solution.py:52
  93.9 1.3 copy.128
  95.8 7.2 %convolution_convert_fusion = bf16[512,4096]{1,0:T(8,128)(2,1)} fusion(bf16[512,4096]{1,0:T(8,128)(2,1)} %param.13, f32[64,8,4,128]{3,2,1,0:T(4,128)S(1)} %bitcast.117, f32[512,512]{1,0:T(8,128)S(1)} %copy-done.9, f32[512,512]{1,0:T(8,128)} %copy.135, f32[512,512]{1,0:T(8,128)} %copy.128, f32[64,8,4,128]{3,2,1,0:T(4,128)S(1)} %bitcast.118), kind=kOutput, calls=%fused_computation | convolution fusion | flops 2150891520 | bytes 13631488 | tf_op jit(solution)/shard_map/dot_general | solution.py:159
  103.0 43.1 %reduce-scatter.2.cloned.1.call-done = bf16[512,1024]{1,0:T(8,128)(2,1)} async-done(((bf16[512,4096]{1,0:T(8,128)(2,1)}), bf16[512,1024]{1,0:T(8,128)(2,1)}) %reduce-scatter.2.cloned.1.call-update) | async-done | bytes 1048592 | tf_op jit(solution)/shard_map/reduce_scatter | solution.py:160
  (77 shorter events, 17.6 us)
Async XLA Ops:
  6.5 3.6 %copy-start.2 = (bf16[512,512]{1,0:T(8,128)(2,1)S(1)}, bf16[512,512]{1,0:T(8,128)(2,1)}, u32[]{:S(2)}) copy-start(bf16[512,512]{1,0:T(8,128)(2,1)} %param.9) | copy-start | bytes 1572868
  6.5 62.9 %all-gather.2.cloned.1.call-start = ((), (), s32[]{:S(2)}) async-start(), calls=%async_computation.1 | async-start | bytes 2359296 | tf_op jit(solution)/shard_map/all_gather | solution.py:130
  14.7 1.0 copy-start.1
  14.8 131.4 %reduce-scatter.2.cloned.1.call-start = ((), (), s32[]{:S(2)}) async-start(), calls=%async_computation.2 | async-start | bytes 5242880 | tf_op jit(solution)/shard_map/reduce_scatter | solution.py:160
  17.0 5.7 %copy-start.10 = (bf16[512,512]{1,0:T(8,128)(2,1)S(1)}, bf16[512,512]{1,0:T(8,128)(2,1)}, u32[]{:S(2)}) copy-start(bf16[512,512]{1,0:T(8,128)(2,1)} %param.7) | copy-start | bytes 1572868
  17.9 69.3 %collective-permute-start = (bf16[2,256,4,128]{3,1,2,0:T(8,128)(2,1)}, bf16[2,256,4,128]{3,1,2,0:T(8,128)(2,1)}, u32[]{:S(2)}, u32[]{:S(2)}) collective-permute-start(bf16[2,256,4,128]{3,1,2,0:T(8,128)(2,1)} %pad_maximum_fusion), channel_id=1, source_target_pairs={{0,4},{4,0},{8,12},{12,8},{16,20},{20,16},{24,28},{28,24},{1,5},{5... | collective-permute-start | bytes 1572872 | tf_op jit(solution)/shard_map/ppermute | solution.py:16
  24.5 1.8 %copy-start.13 = (s32[2]{0:T(128)S(1)}, s32[2]{0:T(128)}, u32[]{:S(2)}) copy-start(s32[2]{0:T(128)} %param.10) | copy-start | bytes 28
  26.3 1.0 copy-start.6
  29.7 3.7 %copy-start.11 = (f32[4]{0:T(128)S(1)}, f32[4]{0:T(128)}, u32[]{:S(2)}) copy-start(f32[4]{0:T(128)} %param.12) | copy-start | bytes 52
  29.7 3.7 %copy-start.12 = (f32[4]{0:T(128)S(1)}, f32[4]{0:T(128)}, u32[]{:S(2)}) copy-start(f32[4]{0:T(128)} %param.11) | copy-start | bytes 52
  31.0 2.4 %copy-start.4 = (f32[2,256,4,128]{3,2,1,0:T(4,128)S(1)}, f32[2,256,4,128]{3,2,1,0:T(4,128)}, u32[]{:S(2)}) copy-start(f32[2,256,4,128]{3,2,1,0:T(4,128)} %reshape.278) | copy-start | bytes 3145732
  33.5 1.6 %copy-start.7 = (bf16[2,256,4,128]{3,2,1,0:T(4,128)(2,1)S(1)}, bf16[2,256,4,128]{3,2,1,0:T(4,128)(2,1)}, u32[]{:S(2)}) copy-start(bf16[2,256,4,128]{3,2,1,0:T(4,128)(2,1)} %reshape_reshape.4) | copy-start | bytes 1572868
  35.8 1.1 copy-start.5
  37.6 1.7 %copy-start.3 = (f32[512,4,128]{2,0,1:T(8,128)S(1)}, f32[512,4,128]{2,0,1:T(8,128)}, u32[]{:S(2)}) copy-start(f32[512,4,128]{2,0,1:T(8,128)} %copy.125) | copy-start | bytes 3145732
  81.7 1.4 copy-start
  93.8 1.9 %copy-start.8 = (f32[2,256,4,128]{3,2,1,0:T(4,128)S(1)}, f32[2,256,4,128]{3,2,1,0:T(4,128)}, u32[]{:S(2)}) copy-start(f32[2,256,4,128]{3,2,1,0:T(4,128)} %copy.121) | copy-start | bytes 3145732
  93.9 1.9 %copy-start.9 = (f32[512,512]{1,0:T(8,128)S(1)}, f32[512,512]{1,0:T(8,128)}, u32[]{:S(2)}) copy-start(f32[512,512]{1,0:T(8,128)} %copy.138) | copy-start | bytes 3145732
Sparse Core Ops, SparseCore 0:
  14.9 54.4 all-gather.1
  103.2 42.9 reduce-scatter.1
where the time goes:
time: 154 us; the launch traced here: 153 us
  waiting for transfers between devices  73 us (47%)
  local copies, waits for them, and re-layouts  25.5 us (17%)
  matrix products  21.7 us (14%)
  other arithmetic  16 us (10%)
  between operations  13.8 us (9%)
  starting transfers between devices  2.98 us (2%)
    reduce_scatter x1, waiting for transfers between devices, per_device(): lax.psum_scatter(terms.astype(jnp.bfloat16), 'head', scatter_dimension=1,...  43.1 us
    all_gather x1, waiting for transfers between devices, per_device(): lax.all_gather(piece.astype(jnp.bfloat16), 'ctx', axis=1, tiled=True)  29.8 us
    dot_general x5, matrix products, attend(): jnp.einsum('gqhd,gkhd->ghqk', grouped, key_rows, preferred_element_type=j...  7.74 us
    dot_general x1, matrix products, per_device(): jnp.dot(attended, final_projection_weights, preferred_element_type=jnp.fl...  7.22 us
    dot_general x5, matrix products, attend(): jnp.einsum('ghqk,gkhd->gqhd', weights.astype(jnp.bfloat16), value_rows, p...  6.78 us
    reshape x3, local copies, waits for them, and re-layouts, attend(): return (numer + update.reshape(numer.shape), denom + totals)  6.45 us
    reshape x3, local copies, waits for them, and re-layouts, per_device(): asking_vectors.astype(jnp.float32)  4.37 us
    reduce_sum x1, other arithmetic, span_means(): return jnp.mean(shaped, axis=2)  3.86 us
  transfers between devices with their start and end apart: 3, of which 2 were waited for; matrix products, arithmetic and copies ran while one was open for 25% of the time, Pallas kernels for 0%

commit v1 on v0

v1 whole, which is shorter than its diff:
```python
import functools
import math

import jax
import jax.numpy as jnp
from jax import lax
from jax.experimental import pallas as pl
from jax.experimental.pallas import tpu as pltpu
from jax.sharding import PartitionSpec as P

EPS = 1e-06
BF16 = jnp.bfloat16
F32 = jnp.float32
TILE = 128
MESH = pl.DeviceIdType.MESH


def dot(a, b):
    return jnp.dot(a, b, preferred_element_type=F32)


def dot_t(a, b):
    return lax.dot_general(a, b, (((1,), (1,)), ((), ())), preferred_element_type=F32)


def unit(rows):
    return rows * lax.rsqrt(jnp.mean(rows * rows, axis=-1, keepdims=True) + EPS)


def kernel(
    n_ctx, n_head, heads, blocks,
    q_hbm, k_hbm, v_hbm, seg, factor, shift, w_hbm,
    out_ref,
    q_raw, k_raw, v_raw, q_s, k_hi, k_lo, acc, att, w_v, y_send, y_recv, own,
    load_sem, kv_send_sem, kv_recv_sem, w_send_sem, w_recv_sem,
    att_send_sem, att_recv_sem, y_send_sem, y_recv_sem, *pieces,
):
    rows, width = q_raw.shape
    dim = width // heads
    block_rows = rows // blocks
    out_cols = out_ref.shape[1]
    steps = n_ctx.bit_length() - 1
    local_levels = blocks.bit_length() - 1
    send, recv = pieces[:steps], pieces[steps:]
    chunks = rows // TILE

    place = lax.axis_index("ctx")
    h = lax.axis_index("head")
    h1 = h + 1 - 2 * (h % 2)
    h2 = (h + 2) % n_head
    h3 = (h1 + 2) % n_head

    k_load = pltpu.make_async_copy(k_hbm, k_raw, load_sem.at[0])
    v_load = pltpu.make_async_copy(v_hbm, v_raw, load_sem.at[1])
    q_load = pltpu.make_async_copy(q_hbm, q_raw, load_sem.at[2])
    k_load.start()
    v_load.start()
    q_load.start()

    barrier = pltpu.get_barrier_semaphore()
    for i in range(1, n_ctx):
        pl.semaphore_signal(
            barrier, inc=1, device_id={"ctx": (place + i) % n_ctx}, device_id_type=MESH
        )
    for peer in (h1, h2):
        pl.semaphore_signal(barrier, inc=1, device_id={"head": peer}, device_id_type=MESH)

    def cols(index):
        return pl.ds(pl.multiple_of(index * out_cols, out_cols), out_cols)

    w_loads = []
    for i, block in enumerate((h, h2)):
        load = pltpu.make_async_copy(
            w_hbm.at[:, cols(block)], w_v.at[i, pl.ds(0, width)], load_sem.at[3 + i]
        )
        load.start()
        w_loads.append(load)

    k_load.wait()

    @pl.loop(0, rows // 64)
    def _(r):
        at = pl.ds(pl.multiple_of(r * 64, 64), 64)
        for a in range(heads):
            c = slice(a * dim, (a + 1) * dim)
            normed = unit(k_raw[at, c].astype(F32))
            high = normed.astype(BF16)
            k_hi[at, c] = high
            k_lo[at, c] = (normed - high.astype(F32)).astype(BF16)

    v_load.wait()
    pl.semaphore_wait(barrier, n_ctx + 1)

    kv_copies = []
    for s in reversed(range(steps)):
        span = 2 ** (local_levels + s)
        count = rows // span
        members = 2**s
        gap = lax.broadcasted_iota(jnp.int32, (count, rows), 1) - span * lax.broadcasted_iota(
            jnp.int32, (count, rows), 0
        )
        average = jnp.where((gap >= 0) & (gap < span), 1.0 / span, 0.0).astype(BF16)
        mean_k = dot(average, k_hi[...]) + dot(average, k_lo[...])
        send[s][:, :width] = mean_k.astype(BF16).astype(send[s].dtype)
        send[s][:, width:] = dot(average, v_raw[...]).astype(BF16).astype(send[s].dtype)
        group = place // members
        sibling = group + 1 - 2 * (group % 2)
        mine = place % members
        for j in range(members):
            copy = pltpu.make_async_remote_copy(
                src_ref=send[s],
                dst_ref=recv[s].at[pl.ds(pl.multiple_of(mine * count, count), count)],
                send_sem=kv_send_sem.at[members - 1 + j],
                recv_sem=kv_recv_sem.at[members - 1 + mine],
                device_id={"ctx": sibling * members + (mine + j) % members},
                device_id_type=MESH,
            )
            copy.start()
            kv_copies.append(copy)

    w_copies = []
    for i, block in enumerate((h1, h3)):
        copy = pltpu.make_async_remote_copy(
            src_ref=w_hbm.at[:, cols(block)],
            dst_ref=w_v.at[i, pl.ds(width, width)],
            send_sem=w_send_sem.at[i],
            recv_sem=w_recv_sem.at[i],
            device_id={"head": h1},
            device_id_type=MESH,
        )
        copy.start()
        w_copies.append(copy)

    q_load.wait()

    @pl.loop(0, rows // 64)
    def _(r):
        at = pl.ds(pl.multiple_of(r * 64, 64), 64)
        for a in range(heads):
            c = slice(a * dim, (a + 1) * dim)
            scale = factor[a] * (math.log2(math.e) / dim)
            q_s[at, c] = (unit(q_raw[at, c].astype(F32)) * scale).astype(BF16)

    ones = jnp.ones((block_rows, dim), BF16)

    def tile(query, keys, values):
        probs = jnp.exp2(dot_t(query, keys)).astype(BF16)
        return dot(probs, jnp.concatenate([values, ones], axis=1))

    for b in range(blocks):
        o = b ^ 1
        keep = jnp.where(seg[b] == seg[o], 1.0, 0.0).astype(F32)
        here = slice(b * block_rows, (b + 1) * block_rows)
        there = slice(o * block_rows, (o + 1) * block_rows)

        @pl.loop(0, block_rows // TILE)
        def _(r):
            at = pl.ds(pl.multiple_of(b * block_rows + r * TILE, TILE), TILE)
            for a in range(heads):
                c = slice(a * dim, (a + 1) * dim)
                query = q_s[at, c]
                acc[a, at, :] = tile(query, k_hi[here, c], v_raw[here, c]) + keep * tile(
                    query, k_hi[there, c], v_raw[there, c]
                )

    def wait_step(s):
        members = 2**s
        count = block_rows // members
        for j in range(members):
            pltpu.make_async_remote_copy(
                src_ref=send[s],
                dst_ref=recv[s].at[pl.ds(j * count, count)],
                send_sem=kv_send_sem.at[members - 1 + j],
                recv_sem=kv_recv_sem.at[members - 1 + j],
                device_id={"ctx": place},
                device_id_type=MESH,
            ).wait_recv()

    def far(s, a, at):
        level = local_levels + s
        c = slice(a * dim, (a + 1) * dim)
        cv = slice(width + a * dim, width + (a + 1) * dim)
        decay = jnp.exp(jnp.full((1, 2 * dim), -level * shift[a], F32))
        keys, values = recv[s][:, c].astype(BF16), recv[s][:, cv].astype(BF16)
        return acc[a, at, :] + decay * tile(q_s[at, c], keys, values)

    for s in reversed(range(1, steps)):
        wait_step(s)

        @pl.loop(0, chunks)
        def _(r):
            at = pl.ds(pl.multiple_of(r * TILE, TILE), TILE)
            for a in range(heads):
                acc[a, at, :] = far(s, a, at)

    wait_step(0)

    def project(r, i):
        at = slice(r * TILE, (r + 1) * TILE)
        return dot(att[0, at, :], w_v[i, :width, :]) + dot(att[1, at, :], w_v[i, width:, :])

    att_copies, y_copies = [], []
    for r in range(chunks + 1):
        if r < chunks:
            at = slice(r * TILE, (r + 1) * TILE)
            for a in range(heads):
                total = far(0, a, at)
                att[0, at, a * dim : (a + 1) * dim] = (total[:, :dim] / total[:, dim:]).astype(BF16)
            copy = pltpu.make_async_remote_copy(
                src_ref=att.at[0, pl.ds(r * TILE, TILE)],
                dst_ref=att.at[1, pl.ds(r * TILE, TILE)],
                send_sem=att_send_sem.at[r],
                recv_sem=att_recv_sem.at[r],
                device_id={"head": h1},
                device_id_type=MESH,
            )
            copy.start()
            att_copies.append(copy)
        if r >= 1:
            if r == 1:
                for i in (1, 0):
                    w_loads[i].wait()
                    w_copies[i].wait_recv()
            att_copies[r - 1].wait_recv()
            at = slice((r - 1) * TILE, r * TILE)
            y_send[at, :] = project(r - 1, 1).astype(BF16)
            copy = pltpu.make_async_remote_copy(
                src_ref=y_send.at[pl.ds((r - 1) * TILE, TILE)],
                dst_ref=y_recv.at[pl.ds((r - 1) * TILE, TILE)],
                send_sem=y_send_sem.at[r - 1],
                recv_sem=y_recv_sem.at[r - 1],
                device_id={"head": h2},
                device_id_type=MESH,
            )
            copy.start()
            y_copies.append(copy)

    for r in range(chunks):
        own[r * TILE : (r + 1) * TILE, :] = project(r, 0)
    for r in range(chunks):
        at = slice(r * TILE, (r + 1) * TILE)
        y_copies[r].wait_recv()
        out_ref[at, :] = (own[at, :] + y_recv[at, :].astype(F32)).astype(BF16)

    for copy in kv_copies + w_copies + att_copies + y_copies:
        copy.wait_send()


def per_device(n_ctx, n_head, q, k, v, seg, factor, shift, weights):
    rows, width = q.shape
    heads = factor.shape[0]
    blocks = seg.shape[0]
    block_rows = rows // blocks
    out_cols = weights.shape[1] // n_head
    steps = n_ctx.bit_length() - 1
    chunks = rows // TILE
    dim = width // heads

    def kind(s):
        return BF16 if (block_rows >> s) % 16 == 0 else F32

    hbm = pl.BlockSpec(memory_space=pltpu.HBM)
    smem = pl.BlockSpec(memory_space=pltpu.SMEM)
    dma = pltpu.SemaphoreType.DMA
    return pl.pallas_call(
        functools.partial(kernel, n_ctx, n_head, heads, blocks),
        out_shape=jax.ShapeDtypeStruct((rows, out_cols), BF16),
        in_specs=[hbm, hbm, hbm, smem, smem, smem, hbm],
        out_specs=pl.BlockSpec(memory_space=pltpu.VMEM),
        scratch_shapes=[
            *[pltpu.VMEM((rows, width), BF16)] * 6,
            pltpu.VMEM((heads, rows, 2 * dim), F32),
            pltpu.VMEM((2, rows, width), BF16),
            pltpu.VMEM((2, 2 * width, out_cols), BF16),
            pltpu.VMEM((rows, out_cols), BF16),
            pltpu.VMEM((rows, out_cols), BF16),
            pltpu.VMEM((rows, out_cols), F32),
            dma((5,)),
            dma((n_ctx - 1,)),
            dma((n_ctx - 1,)),
            dma((2,)),
            dma((2,)),
            dma((chunks,)),
            dma((chunks,)),
            dma((chunks,)),
            dma((chunks,)),
            *[pltpu.VMEM((block_rows >> s, 2 * width), kind(s)) for s in range(steps)],
            *[pltpu.VMEM((block_rows, 2 * width), kind(s)) for s in range(steps)],
        ],
        compiler_params=pltpu.CompilerParams(
            collective_id=0, has_side_effects=True, vmem_limit_bytes=48 * 1024 * 1024
        ),
        cost_estimate=pl.CostEstimate(
            flops=4 * 10**9, bytes_accessed=8 * 10**6, transcendentals=3 * 10**6
        ),
    )(q, k, v, seg, factor, shift, weights)


def solution(mesh):
    placed = (
        P("ctx", "head"),
        P("ctx", "head"),
        P("ctx", "head"),
        P("ctx"),
        P("head"),
        P("head"),
        P("head", None),
    )
    body = functools.partial(per_device, mesh.shape["ctx"], mesh.shape["head"])
    return jax.shard_map(
        body, mesh=mesh, in_specs=placed, out_specs=P("ctx", "head"), check_vma=False
    )
```

time: 154 us -> 67.9 us (0.44)
  waiting for transfers between devices: 73 us -> 0 us
  Pallas kernels: 0 us -> 61 us
  matrix products: 21.7 us -> 0 us
  local copies, waits for them, and re-layouts: 25.5 us -> 6.06 us
  other arithmetic: 16 us -> 0 us
  between operations: 13.8 us -> 0.02 us
  starting transfers between devices: 2.98 us -> 0 us
    pallas_call x0 -> x1, Pallas kernels: none -> 61 us  [per_device(): pl.pallas_call(functools.partial(kernel, n_ctx, n_head, heads, blocks), o...]
    reduce_scatter x1 -> x0, waiting for transfers between devices: 43.1 us -> none  [per_device(): lax.psum_scatter(terms.astype(jnp.bfloat16), 'head', scatter_dimension=1,...]
    all_gather x1 -> x0, waiting for transfers between devices: 29.8 us -> none  [per_device(): lax.all_gather(piece.astype(jnp.bfloat16), 'ctx', axis=1, tiled=True)]
    dot_general x11 -> x0, matrix products: 21.7 us -> none  [the longest x5 7.74 us: attend(): jnp.einsum('gqhd,gkhd->ghqk', grouped, key_rows, preferred_element_type=j...]
    reshape x11 -> x0, local copies, waits for them, and re-layouts: 14.3 us -> none  [the longest x3 6.45 us: attend(): return (numer + update.reshape(numer.shape), denom + totals)]
    reduce_sum x7 -> x0, other arithmetic: 7.2 us -> none  [the longest x1 3.86 us: span_means(): return jnp.mean(shaped, axis=2)]
    convert_element_type x6 -> x0, other arithmetic: 4.81 us -> none  [the longest x1 1.86 us: per_device(): lax.all_gather(piece.astype(jnp.bfloat16), 'ctx', axis=1, tiled=True)]
    unnamed x30 -> x13, local copies, waits for them, and re-layouts: 2.16 us -> 6.06 us
  transfers between devices with their start and end apart: 3 -> 0, of which waited for: 2 -> 0; matrix products, arithmetic and copies ran while one was open for 25% -> 0% of each run, Pallas kernels for 0% -> 0%
where the time goes in v1:
time: 67.9 us; the launch traced here: 67.1 us
  Pallas kernels  61 us (90%)
  local copies, waits for them, and re-layouts  6.06 us (9%)
    pallas_call x1, Pallas kernels, per_device(): pl.pallas_call(functools.partial(kernel, n_ctx, n_head, heads, blocks), o...  61 us
    unnamed x13, local copies, waits for them, and re-layouts  6.06 us

profile of v1, /device:TPU:0, one launch (start us, length us, event | category | flops | bytes accessed | tf_op | source)
XLA Modules:
  0.0 67.1 jit_solution(18074882894807236315)
XLA Ops:
  0.0 0.0 copy-start
  0.0 1.0 %copy-done = bf16[512,512]{1,0:T(8,128)(2,1)S(1)} copy-done((bf16[512,512]{1,0:T(8,128)(2,1)S(1)}, bf16[512,512]{1,0:T(8,128)(2,1)}, u32[]{:S(2)}) %copy-start) | copy-done | bytes 524312
  1.0 0.0 copy-start.1
  1.0 1.0 %copy-done.1 = bf16[512,512]{1,0:T(8,128)(2,1)S(1)} copy-done((bf16[512,512]{1,0:T(8,128)(2,1)S(1)}, bf16[512,512]{1,0:T(8,128)(2,1)}, u32[]{:S(2)}) %copy-start.1) | copy-done | bytes 524312
  2.1 0.0 copy-start.2
  2.1 1.0 %copy-done.2 = bf16[512,512]{1,0:T(8,128)(2,1)S(1)} copy-done((bf16[512,512]{1,0:T(8,128)(2,1)S(1)}, bf16[512,512]{1,0:T(8,128)(2,1)}, u32[]{:S(2)}) %copy-start.2) | copy-done | bytes 524312
  3.1 0.0 copy-start.3
  3.1 0.7 copy-done.3
  3.8 0.0 copy-start.4
  3.8 0.7 copy-done.4
  4.4 0.0 copy-start.5
  4.4 0.7 copy-done.5
  5.1 61.0 %shard_map.73 = bf16[512,1024]{1,0:T(8,128)(2,1)S(1)} custom-call(bf16[512,512]{1,0:T(8,128)(2,1)S(1)} %copy-done, bf16[512,512]{1,0:T(8,128)(2,1)S(1)} %copy-done.1, bf16[512,512]{1,0:T(8,128)(2,1)S(1)} %copy-done.2, s32[2]{0:T(128)S(1)} %copy-done.3, f32[4]{0:T(128)S(1)} %copy-done.4, f32[4]{0:T(128)S(1)} %copy-done.5, bf16[512,4096]{1,0:T(8,128)(2,1)} %w_hbm.1), custom_call_target="tpu_custom_call" | custom-call | flops 4000000000 | bytes 8000000 | tf_op jit(solution)/shard_map/pallas_call | solution.py:265
  66.1 1.0 %copy.9 = bf16[512,1024]{1,0:T(8,128)(2,1)} copy(bf16[512,1024]{1,0:T(8,128)(2,1)S(1)} %shard_map.73) | data formatting | bytes 2097152
Async XLA Ops:
  0.0 1.0 %copy-start = (bf16[512,512]{1,0:T(8,128)(2,1)S(1)}, bf16[512,512]{1,0:T(8,128)(2,1)}, u32[]{:S(2)}) copy-start(bf16[512,512]{1,0:T(8,128)(2,1)} %q_hbm.1) | copy-start | bytes 1572868
  1.0 1.0 %copy-start.1 = (bf16[512,512]{1,0:T(8,128)(2,1)S(1)}, bf16[512,512]{1,0:T(8,128)(2,1)}, u32[]{:S(2)}) copy-start(bf16[512,512]{1,0:T(8,128)(2,1)} %k_hbm.1) | copy-start | bytes 1572868
  2.1 1.0 %copy-start.2 = (bf16[512,512]{1,0:T(8,128)(2,1)S(1)}, bf16[512,512]{1,0:T(8,128)(2,1)}, u32[]{:S(2)}) copy-start(bf16[512,512]{1,0:T(8,128)(2,1)} %v_hbm.1) | copy-start | bytes 1572868
  3.1 0.7 copy-start.3
  3.8 0.7 copy-start.4
  4.4 0.7 copy-start.5

commit v2 on v1

v2 whole, which is shorter than its diff:
```python
import functools
import math

import jax
import jax.numpy as jnp
from jax import lax
from jax.experimental import pallas as pl
from jax.experimental.pallas import tpu as pltpu
from jax.sharding import PartitionSpec as P

EPS = 1e-06
BF16 = jnp.bfloat16
F32 = jnp.float32
TILE = 128
MESH = pl.DeviceIdType.MESH


def dot(a, b):
    return jnp.dot(a, b, preferred_element_type=F32)


def dot_t(a, b):
    return lax.dot_general(a, b, (((1,), (1,)), ((), ())), preferred_element_type=F32)


def flipped(index, bit):
    size = 2**bit
    return index + size - 2 * size * ((index // size) % 2)


def unit(rows):
    dim = rows.shape[1]
    squares = rows * rows
    high = squares.astype(BF16)
    low = (squares - high.astype(F32)).astype(BF16)
    total = dot(jnp.concatenate([high, low], axis=1), jnp.ones((2 * dim, dim), BF16))
    return rows * lax.rsqrt(total * (1.0 / dim) + EPS)


def row_chunks(rows):
    half = TILE // 2
    sizes = [half, half] + [TILE] * (rows // TILE - 2) + [half, half]
    return [(sum(sizes[:i]), size) for i, size in enumerate(sizes)]


def kernel(
    n_ctx, n_head, heads, blocks,
    q_hbm, k_hbm, v_hbm, seg, factor, shift, w_hbm,
    out_ref,
    q_raw, k_raw, v_raw, q_s, k_hi, average, acc, att, w_v, y_send, y_recv, own,
    load_sem, kv_send_sem, kv_recv_sem, w_send_sem, w_recv_sem,
    att_send_sem, att_recv_sem, y_send_sem, y_recv_sem, *pieces,
):
    rows, width = q_raw.shape
    dim = width // heads
    block_rows = rows // blocks
    out_cols = out_ref.shape[1]
    steps = n_ctx.bit_length() - 1
    local_levels = blocks.bit_length() - 1
    send, recv = pieces[:steps], pieces[steps:]
    chunks = row_chunks(rows)

    place = lax.axis_index("ctx")
    h = lax.axis_index("head")
    h1 = h + 1 - 2 * (h % 2)
    h2 = (h + 2) % n_head
    h3 = (h1 + 2) % n_head

    k_load = pltpu.make_async_copy(k_hbm, k_raw, load_sem.at[0])
    v_load = pltpu.make_async_copy(v_hbm, v_raw, load_sem.at[1])
    q_load = pltpu.make_async_copy(q_hbm, q_raw, load_sem.at[2])
    k_load.start()
    v_load.start()
    q_load.start()

    barrier = pltpu.get_barrier_semaphore()
    for bit in range(steps):
        pl.semaphore_signal(
            barrier, inc=1, device_id={"ctx": flipped(place, bit)}, device_id_type=MESH
        )
    for peer in (h1, h2):
        pl.semaphore_signal(barrier, inc=1, device_id={"head": peer}, device_id_type=MESH)

    def cols(index):
        return pl.ds(pl.multiple_of(index * out_cols, out_cols), out_cols)

    w_loads = []
    for i, block in enumerate((h, h2)):
        load = pltpu.make_async_copy(
            w_hbm.at[:, cols(block)], w_v.at[i, pl.ds(0, width)], load_sem.at[3 + i]
        )
        load.start()
        w_loads.append(load)

    tops = [sum(rows >> (local_levels + i) for i in range(s)) for s in range(steps)]
    for s in range(steps):
        span = 2 ** (local_levels + s)
        count = rows // span
        token = lax.broadcasted_iota(jnp.int32, (count, rows), 1)
        first = span * lax.broadcasted_iota(jnp.int32, (count, rows), 0)
        gap = token - first
        average[tops[s] : tops[s] + count, :] = jnp.where(
            (gap >= 0) & (gap < span), 1.0 / span, 0.0
        ).astype(BF16)

    k_load.wait()
    for r in range(0, rows, TILE):
        for a in range(heads):
            c = slice(a * dim, (a + 1) * dim)
            k_hi[r : r + TILE, c] = unit(k_raw[r : r + TILE, c].astype(F32)).astype(BF16)

    v_load.wait()
    pl.semaphore_wait(barrier, steps + 2)

    kv_copies = {}

    def hop(s, stage, src, first_row, count, bit):
        spot = s * (s + 1) // 2 + stage
        copy = pltpu.make_async_remote_copy(
            src_ref=src,
            dst_ref=recv[s].at[pl.ds(pl.multiple_of(first_row, count), count)],
            send_sem=kv_send_sem.at[spot],
            recv_sem=kv_recv_sem.at[spot],
            device_id={"ctx": flipped(place, bit)},
            device_id_type=MESH,
        )
        copy.start()
        kv_copies[s, stage] = copy

    def forward(s, stage):
        kv_copies[s, stage].wait_recv()
        size = 2**stage
        count = size * (block_rows >> s)
        first_row = (place % 2**s) // size * count
        held = recv[s].at[pl.ds(pl.multiple_of(first_row, count), count)]
        hop(s, stage + 1, held, first_row, count, stage)

    for s in reversed(range(steps)):
        count = block_rows >> s
        matrix = average[tops[s] : tops[s] + count, :]
        send[s][:, :width] = dot(matrix, k_hi[...]).astype(BF16).astype(send[s].dtype)
        send[s][:, width:] = dot(matrix, v_raw[...]).astype(BF16).astype(send[s].dtype)
        hop(s, 0, send[s], (place % 2**s) * count, count, s)

    w_copies = []
    for i, block in enumerate((h1, h3)):
        copy = pltpu.make_async_remote_copy(
            src_ref=w_hbm.at[:, cols(block)],
            dst_ref=w_v.at[i, pl.ds(width, width)],
            send_sem=w_send_sem.at[i],
            recv_sem=w_recv_sem.at[i],
            device_id={"head": h1},
            device_id_type=MESH,
        )
        copy.start()
        w_copies.append(copy)

    q_load.wait()

    for r in range(0, rows, TILE):
        for a in range(heads):
            c = slice(a * dim, (a + 1) * dim)
            scale = factor[a] * (math.log2(math.e) / dim)
            q_s[r : r + TILE, c] = (unit(q_raw[r : r + TILE, c].astype(F32)) * scale).astype(BF16)

    ones = jnp.ones((block_rows, dim), BF16)

    def tile(query, keys, values):
        probs = jnp.exp2(dot_t(query, keys)).astype(BF16)
        return dot(probs, jnp.concatenate([values, ones], axis=1))

    for b in range(blocks):
        o = b ^ 1
        keep = jnp.where(seg[b] == seg[o], 1.0, 0.0).astype(F32)
        here = slice(b * block_rows, (b + 1) * block_rows)
        there = slice(o * block_rows, (o + 1) * block_rows)

        @pl.loop(0, block_rows // TILE)
        def _(r):
            at = pl.ds(pl.multiple_of(b * block_rows + r * TILE, TILE), TILE)
            for a in range(heads):
                c = slice(a * dim, (a + 1) * dim)
                query = q_s[at, c]
                acc[a, at, :] = tile(query, k_hi[here, c], v_raw[here, c]) + keep * tile(
                    query, k_hi[there, c], v_raw[there, c]
                )

        if b == 0:
            for s in reversed(range(2, steps)):
                forward(s, 0)

    def far(s, a, at):
        level = local_levels + s
        c = slice(a * dim, (a + 1) * dim)
        cv = slice(width + a * dim, width + (a + 1) * dim)
        decay = jnp.exp(jnp.full((1, 2 * dim), -level * shift[a], F32))
        keys, values = recv[s][:, c].astype(BF16), recv[s][:, cv].astype(BF16)
        return acc[a, at, :] + decay * tile(q_s[at, c], keys, values)

    if steps > 1:
        forward(1, 0)
    for stage in range(1, steps):
        for s in reversed(range(stage + 1, steps)):
            forward(s, stage)
    last = min(1, steps - 1)
    for s in [s for s in [0, *reversed(range(2, steps))] if s != last]:
        kv_copies[s, s].wait_recv()

        @pl.loop(0, rows // TILE)
        def _(r):
            at = pl.ds(pl.multiple_of(r * TILE, TILE), TILE)
            for a in range(heads):
                acc[a, at, :] = far(s, a, at)

    kv_copies[last, last].wait_recv()

    def project(at, i):
        return dot(att[0, at, :], w_v[i, :width, :]) + dot(att[1, at, :], w_v[i, width:, :])

    att_copies, y_copies = [], []
    for r in range(len(chunks) + 1):
        if r < len(chunks):
            first, size = chunks[r]
            at = slice(first, first + size)
            for a in range(heads):
                total = far(last, a, at)
                att[0, at, a * dim : (a + 1) * dim] = (total[:, :dim] / total[:, dim:]).astype(BF16)
            copy = pltpu.make_async_remote_copy(
                src_ref=att.at[0, pl.ds(first, size)],
                dst_ref=att.at[1, pl.ds(first, size)],
                send_sem=att_send_sem.at[r],
                recv_sem=att_recv_sem.at[r],
                device_id={"head": h1},
                device_id_type=MESH,
            )
            copy.start()
            att_copies.append(copy)
        if r >= 1:
            if r == 1:
                for i in (1, 0):
                    w_loads[i].wait()
                    w_copies[i].wait_recv()
            att_copies[r - 1].wait_recv()
            first, size = chunks[r - 1]
            at = slice(first, first + size)
            y_send[at, :] = project(at, 1).astype(BF16)
            copy = pltpu.make_async_remote_copy(
                src_ref=y_send.at[pl.ds(first, size)],
                dst_ref=y_recv.at[pl.ds(first, size)],
                send_sem=y_send_sem.at[r - 1],
                recv_sem=y_recv_sem.at[r - 1],
                device_id={"head": h2},
                device_id_type=MESH,
            )
            copy.start()
            y_copies.append(copy)

    for first in range(0, rows, TILE):
        at = slice(first, first + TILE)
        own[at, :] = project(at, 0)
    for (first, size), copy in zip(chunks, y_copies):
        at = slice(first, first + size)
        copy.wait_recv()
        out_ref[at, :] = (own[at, :] + y_recv[at, :].astype(F32)).astype(BF16)

    for copy in list(kv_copies.values()) + w_copies + att_copies + y_copies:
        copy.wait_send()


def per_device(n_ctx, n_head, q, k, v, seg, factor, shift, weights):
    rows, width = q.shape
    heads = factor.shape[0]
    blocks = seg.shape[0]
    block_rows = rows // blocks
    out_cols = weights.shape[1] // n_head
    steps = n_ctx.bit_length() - 1
    chunks = len(row_chunks(rows))
    dim = width // heads
    hops = steps * (steps + 1) // 2

    def kind(s):
        return BF16 if (block_rows >> s) % 16 == 0 else F32

    hbm = pl.BlockSpec(memory_space=pltpu.HBM)
    smem = pl.BlockSpec(memory_space=pltpu.SMEM)
    dma = pltpu.SemaphoreType.DMA
    return pl.pallas_call(
        functools.partial(kernel, n_ctx, n_head, heads, blocks),
        out_shape=jax.ShapeDtypeStruct((rows, out_cols), BF16),
        in_specs=[hbm, hbm, hbm, smem, smem, smem, hbm],
        out_specs=pl.BlockSpec(memory_space=pltpu.VMEM),
        scratch_shapes=[
            *[pltpu.VMEM((rows, width), BF16)] * 5,
            pltpu.VMEM((rows, rows), BF16),
            pltpu.VMEM((heads, rows, 2 * dim), F32),
            pltpu.VMEM((2, rows, width), BF16),
            pltpu.VMEM((2, 2 * width, out_cols), BF16),
            pltpu.VMEM((rows, out_cols), BF16),
            pltpu.VMEM((rows, out_cols), BF16),
            pltpu.VMEM((rows, out_cols), F32),
            dma((5,)),
            dma((hops,)),
            dma((hops,)),
            dma((2,)),
            dma((2,)),
            dma((chunks,)),
            dma((chunks,)),
            dma((chunks,)),
            dma((chunks,)),
            *[pltpu.VMEM((block_rows >> s, 2 * width), kind(s)) for s in range(steps)],
            *[pltpu.VMEM((block_rows, 2 * width), kind(s)) for s in range(steps)],
        ],
        compiler_params=pltpu.CompilerParams(
            collective_id=0, has_side_effects=True, vmem_limit_bytes=64 * 1024 * 1024 - 65536
        ),
        cost_estimate=pl.CostEstimate(
            flops=4 * 10**9, bytes_accessed=8 * 10**6, transcendentals=3 * 10**6
        ),
    )(q, k, v, seg, factor, shift, weights)


def solution(mesh):
    placed = (
        P("ctx", "head"),
        P("ctx", "head"),
        P("ctx", "head"),
        P("ctx"),
        P("head"),
        P("head"),
        P("head", None),
    )
    body = functools.partial(per_device, mesh.shape["ctx"], mesh.shape["head"])
    return jax.shard_map(
        body, mesh=mesh, in_specs=placed, out_specs=P("ctx", "head"), check_vma=False
    )
```

time: 67.9 us -> 61.1 us (0.90)
  local copies, waits for them, and re-layouts: 6.06 us -> 2.26 us
  Pallas kernels: 61 us -> 58.6 us
    unnamed x13 -> x1, local copies, waits for them, and re-layouts: 6.06 us -> 2.26 us
    pallas_call x1, Pallas kernels: 61 us -> 58.6 us  [per_device(): pl.pallas_call(functools.partial(kernel, n_ctx, n_head, heads, blocks), o...]
where the time goes in v2:
time: 61.1 us; the launch traced here: 60.9 us
  Pallas kernels  58.6 us (96%)
  local copies, waits for them, and re-layouts  2.26 us (4%)
    pallas_call x1, Pallas kernels, per_device(): pl.pallas_call(functools.partial(kernel, n_ctx, n_head, heads, blocks), o...  58.6 us
    unnamed x1, local copies, waits for them, and re-layouts  2.26 us

profile of v2, /device:TPU:0, one launch (start us, length us, event | category | flops | bytes accessed | tf_op | source)
XLA Modules:
  0.0 60.9 jit_solution(12685439845542284968)
XLA Ops:
  0.0 58.6 %shard_map.73 = bf16[512,1024]{1,0:T(8,128)(2,1)} custom-call(bf16[512,512]{1,0:T(8,128)(2,1)} %q_hbm.1, bf16[512,512]{1,0:T(8,128)(2,1)} %k_hbm.1, bf16[512,512]{1,0:T(8,128)(2,1)} %v_hbm.1, s32[2]{0:T(128)} %seg.1, f32[4]{0:T(128)} %factor.1, f32[4]{0:T(128)} %shift.1, bf16[512,4096]{1,0:T(8,128)(2,1)} %w_hbm.1), custom_call_target="tpu_custom_call" | custom-call | flops 4000000000 | bytes 8000000 | tf_op jit(solution)/shard_map/pallas_call | solution.py:287
  58.6 2.3 %copy.9 = bf16[512,1024]{1,0:T(8,128)(2,1)} copy(bf16[512,1024]{1,0:T(8,128)(2,1)} %shard_map.73) | data formatting | bytes 2097152

commit v3 on v2

--- a/solution.py
+++ b/solution.py
@@ -135,7 +135,7 @@
         held = recv[s].at[pl.ds(pl.multiple_of(first_row, count), count)]
         hop(s, stage + 1, held, first_row, count, stage)
 
-    for s in reversed(range(steps)):
+    for s in range(steps):
         count = block_rows >> s
         matrix = average[tops[s] : tops[s] + count, :]
         send[s][:, :width] = dot(matrix, k_hi[...]).astype(BF16).astype(send[s].dtype)

time: 61.1 us -> 60.7 us (level)
  no operation moved by 1% of the time
where the time goes in v3:
time: 60.7 us; the launch traced here: 60.6 us
  Pallas kernels  58.3 us (96%)
  local copies, waits for them, and re-layouts  2.26 us (4%)
    pallas_call x1, Pallas kernels, per_device(): pl.pallas_call(functools.partial(kernel, n_ctx, n_head, heads, blocks), o...  58.3 us
    unnamed x1, local copies, waits for them, and re-layouts  2.26 us

profile of v3, /device:TPU:0, one launch (start us, length us, event | category | flops | bytes accessed | tf_op | source)
XLA Modules:
  0.0 60.6 jit_solution(18099227810293402623)
XLA Ops:
  0.0 58.3 %shard_map.73 = bf16[512,1024]{1,0:T(8,128)(2,1)} custom-call(bf16[512,512]{1,0:T(8,128)(2,1)} %q_hbm.1, bf16[512,512]{1,0:T(8,128)(2,1)} %k_hbm.1, bf16[512,512]{1,0:T(8,128)(2,1)} %v_hbm.1, s32[2]{0:T(128)} %seg.1, f32[4]{0:T(128)} %factor.1, f32[4]{0:T(128)} %shift.1, bf16[512,4096]{1,0:T(8,128)(2,1)} %w_hbm.1), custom_call_target="tpu_custom_call" | custom-call | flops 4000000000 | bytes 8000000 | tf_op jit(solution)/shard_map/pallas_call | solution.py:287
  58.3 2.3 %copy.9 = bf16[512,1024]{1,0:T(8,128)(2,1)} copy(bf16[512,1024]{1,0:T(8,128)(2,1)} %shard_map.73) | data formatting | bytes 2097152
